TPU v7x, 128 devices: a whole 4x4x4 slice. The times are simulated.
128 devices in a mesh: ha: 8 (over x, y_lo), wa: 16 (over y_hi, z, core).
Axes of the slice: x: 4, y: 4 (y_hi: 2, y_lo: 2; y = y_hi * 2 + y_lo), z: 4, core: 2. Of those that a mesh axis runs over, the one named last changes fastest.
Arguments:
- latent: bfloat16 [16, 32, 128, 320], P(None, 'ha', 'wa'), may hold values from -40 to 40, as said below
- cotangent: bfloat16 [16, 32, 128, 320], P(None, 'ha', 'wa'), may hold values from -40 to 40, as said below
- w_fine: bfloat16 [9, 320, 320], replicated, may hold values from -0.109375 to 0.109375
- w_down: bfloat16 [4, 320, 640], replicated, may hold values from -0.15625 to 0.15625
- w_coarse: bfloat16 [9, 640, 640], replicated, may hold values from -0.078125 to 0.078125
- w_up: bfloat16 [4, 640, 320], replicated, may hold values from -0.25 to 0.25
Outputs:
- output: bfloat16 [16, 32, 128, 320], P(None, 'ha', 'wa')
- grad_latent: bfloat16 [16, 32, 128, 320], P(None, 'ha', 'wa')
- grad_fine: float32 [9, 320, 320], P(None, 'ha', 'wa')
- grad_down: float32 [4, 320, 640], P(None, 'ha', 'wa')
- grad_coarse: float32 [9, 640, 640], P(None, 'ha', 'wa')
- grad_up: float32 [4, 640, 320], P(None, 'ha', 'wa')
Inputs may be any that keep to these rules, and one draw needn't show every extreme that they name: `latent`: finite activations of order one. `cotangent`: finite gradients.
All inputs are finite; a program needn't handle non-finite values.
Results may differ from a plain program's by a relative error of at most 0.014.
Values may be sent and summed in bfloat16 or wider, within the bound.
No kernel may reach another device: no remote copies, remote signals or barrier semaphores. Data moves between devices by JAX's collectives and lax.ppermute only.
A program may use at most 192 MiB of HBM per device.

v0:
```python
import functools

import jax
import jax.numpy as jnp
from jax import lax
from jax.experimental import pallas as pl
from jax.experimental.pallas import tpu as pltpu
from jax.sharding import PartitionSpec as P


BF = jnp.bfloat16
F32 = jnp.float32
EPS = 1e-05
C1, C2 = 320, 640
B = 64
COUNT = 32.0 * 128.0 * 10.0
VMEM = 16 * 1024 * 1024


def nn(a, b):
    return lax.dot_general(a, b, (((1,), (0,)), ((), ())), preferred_element_type=F32)


def nt(a, b):
    return lax.dot_general(a, b, (((1,), (1,)), ((), ())), preferred_element_type=F32)


def tn(a, b):
    return lax.dot_general(a, b, (((0,), (0,)), ((), ())), preferred_element_type=F32)


def iota(shape, dim):
    return lax.broadcasted_iota(jnp.int32, shape, dim)


def one_hot(cond):
    return jnp.where(cond, 1.0, 0.0).astype(BF)


def arrival_of(q):
    row, par, col = (q >> 7, (q >> 6) & 1, q & 63)
    return ((col >> 2) << 5) + (row << 3) + ((col & 3) << 1) + par


def to_parity(which):
    q, a = (iota((512, 1024), 0), iota((512, 1024), 1))
    return one_hot((arrival_of(q) == ((a >> 6) << 5) + (a & 31)) & (((a >> 5) & 1) == which))


def from_parity():
    return one_hot(arrival_of(iota((512, 512), 1)) == iota((512, 512), 0))


def prev_col(v):
    return jnp.where(iota(v.shape, 0) == 0, 0.0, pltpu.roll(v, 1, 0))


def next_col(v):
    return jnp.where(iota(v.shape, 0) == B - 1, 0.0, pltpu.roll(v, B - 1, 0))


def group_sums(sums):
    same = ((iota((C1, C1), 0) * 6554) >> 16) == ((iota((C1, C1), 1) * 6554) >> 16)
    return lax.dot_general(
        sums,
        jnp.where(same, 1.0, 0.0).astype(F32),
        (((1,), (0,)), ((), ())),
        precision=lax.Precision.HIGHEST,
        preferred_element_type=F32,
    )


def group_sums(sums):
    same = ((iota((C1, C1), 0) * 6554) >> 16) == ((iota((C1, C1), 1) * 6554) >> 16)
    return lax.dot_general(
        sums,
        jnp.where(same, 1.0, 0.0).astype(F32),
        (((1,), (0,)), ((), ())),
        precision=lax.Precision.HIGHEST,
        preferred_element_type=F32,
    )


def norm_of(st_ref):
    totals = group_sums(st_ref[...]) / COUNT
    mean = totals[0:1]
    return mean, lax.rsqrt(totals[1:2] - mean * mean + EPS)


def sigmoid(v):
    return 1.0 / (1.0 + jnp.exp(-v))


def silu_grad(v):
    s = sigmoid(v)
    return s * (1.0 + v * (1.0 - s))


def rows8(a, b):
    return jnp.concatenate([a, b, jnp.zeros((6, a.shape[1]), F32)], axis=0)


def call(kernel, outs, n_in, scratch=(), smem=0, us=2, after=(), vmem=VMEM):
    first = smem + n_in

    def body(*refs):
        kernel(*refs[:first], *refs[first + len(after) :])

    f = pl.pallas_call(
        body,
        out_shape=outs,
        in_specs=[pl.BlockSpec(memory_space=pltpu.SMEM)] * smem
        + [pl.BlockSpec(memory_space=pltpu.VMEM)] * n_in
        + [pl.BlockSpec(memory_space=pl.ANY)] * len(after),
        out_specs=jax.tree.map(lambda _: pl.BlockSpec(memory_space=pltpu.VMEM), outs),
        scratch_shapes=list(scratch),
        compiler_params=pltpu.CompilerParams(vmem_limit_bytes=vmem),
        cost_estimate=pl.CostEstimate(flops=us * 10**9, bytes_accessed=10**6, transcendentals=0),
    )
    return lambda *args: f(*args, *after)


def sds(shape, dtype=BF):
    return jax.ShapeDtypeStruct(shape, dtype)


def turn_kernel(count, *refs):
    for src, dst in zip(refs[:count], refs[-count - 1 : -1]):
        dst[0] = jnp.transpose(src[0])
    refs[-1][...] = jnp.zeros((8, 128), F32)


def turned(weights, us, after=()):
    def spec(rows, cols):
        return pl.BlockSpec((1, rows, cols), lambda t: (t, 0, 0))

    outs = [(w.shape[0], w.shape[2], w.shape[1]) for w in weights]
    return pl.pallas_call(
        functools.partial(turn_kernel, len(weights)),
        grid=(weights[0].shape[0],),
        out_shape=[sds(o) for o in outs] + [sds((8, 128), F32)],
        in_specs=[spec(*w.shape[1:]) for w in weights] + [pl.BlockSpec(memory_space=pl.ANY)] * len(after),
        out_specs=[spec(*o[1:]) for o in outs] + [pl.BlockSpec((8, 128), lambda t: (0, 0))],
        compiler_params=pltpu.CompilerParams(vmem_limit_bytes=VMEM),
        cost_estimate=pl.CostEstimate(flops=us * 10**9, bytes_accessed=10**6, transcendentals=0),
    )(*weights, *after)


def sort_kernel(a_ref, wu, x_ref, up_ref, down_ref, cot_ref, g_ref, st_ref):
    x = nn(to_parity(0), a_ref[...])
    c = nn(to_parity(1), a_ref[...]).astype(BF)
    xb = x.astype(BF)
    x_ref[...] = xb
    for k in range(4):
        for h in range(2):
            at = (2 * h + k // 2) * 128 + (k % 2) * B
            cot_ref[h * B : h * B + B, k * C1 : (k + 1) * C1] = c[at : at + B]
    g = nn(cot_ref[...], wu[...]).astype(BF)
    g_ref[...] = g
    up_ref[0:384, :] = xb[0:384]
    up_ref[384:448, :] = g[0:B, 0:C1]
    up_ref[448:512, :] = g[0:B, C1:C2]
    down_ref[0:384, :] = xb[128:512]
    down_ref[384:448, :] = g[B : 2 * B, 0:C1]
    down_ref[448:512, :] = g[B : 2 * B, C1:C2]
    st_ref[...] = rows8(jnp.sum(x, axis=0, keepdims=True), jnp.sum(x * x, axis=0, keepdims=True))


def forward_kernel(
    edge, x_ref, xd_ref, xu_ref, st_ref, wf, wd,
    ave_ref, avo_ref, low_ref, cact_ref, depth_ref, cv,
    ve, vo, d,
):
    mean, rstd = norm_of(st_ref)
    in_top = jnp.where(edge[0] == 1, 0.0, 1.0)
    in_bot = jnp.where(edge[1] == 1, 0.0, 1.0)

    def latent(row, par):
        ref, base = (xd_ref, row + 3) if row < 0 else (x_ref, row) if row < 4 else (xu_ref, row - 4)
        return ref[base * 128 + par * B : base * 128 + par * B + B, :].astype(F32)

    for row in range(-3, 7):
        at = slice((row + 3) * B, (row + 4) * B)
        for par in range(2):
            z = (latent(row, par) - mean) * rstd
            act = z * sigmoid(z)
            if row < 0:
                act = act * in_top
            if row > 3:
                act = act * in_bot
            ab = act.astype(BF)
            if par == 0:
                ve[at, C1 : 2 * C1] = ab
                vo[at, 0:C1] = ab
                vo[at, 2 * C1 : 3 * C1] = next_col(act).astype(BF)
            else:
                ve[at, 2 * C1 : 3 * C1] = ab
                vo[at, C1 : 2 * C1] = ab
                ve[at, 0:C1] = prev_col(act).astype(BF)

    ave_ref[...] = ve[2 * B : 8 * B, :]
    avo_ref[...] = vo[2 * B : 8 * B, :]
    for par, v in ((0, ve), (1, vo)):
        acc = nn(v[0:512, :], wf[0]) + nn(v[B : B + 512, :], wf[1]) + nn(v[2 * B : 2 * B + 512, :], wf[2])
        for rr in range(8):
            k = 2 * (rr % 2) + par
            r = latent(rr - 2, par) + acc[rr * B : rr * B + B]
            d[(rr // 2) * B : (rr // 2) * B + B, k * C1 : (k + 1) * C1] = r.astype(BF)
    depth_ref[...] = d[B : 3 * B, :]

    low = nn(d[...], wd[...]).astype(BF)
    low_ref[...] = low[B : 3 * B]
    for h in range(4):
        lf = low[h * B : h * B + B].astype(F32)
        ca = lf * sigmoid(lf)
        if h == 0:
            ca = ca * in_top
        if h == 3:
            ca = ca * in_bot
        s = slice(h * B, h * B + B)
        cv[s, 0:C2] = prev_col(ca).astype(BF)
        cv[s, C2 : 2 * C2] = ca.astype(BF)
        cv[s, 2 * C2 : 3 * C2] = next_col(ca).astype(BF)
    cact_ref[...] = cv[B : 3 * B, C2 : 2 * C2]


def coarse_level_kernel(cv, low_ref, depth_ref, wc, wu, send_ref, coarse_ref, ox):
    acc = low_ref[...].astype(F32)
    for i in range(3):
        acc = acc + nn(cv[i * B : i * B + 128, :], wc[i])
    coarse = acc.astype(BF)
    coarse_ref[...] = coarse
    for k in range(4):
        up = nn(coarse, wu[k])
        for h in range(2):
            at = (2 * h + k // 2) * 128 + (k % 2) * B
            o = depth_ref[h * B : h * B + B, k * C1 : (k + 1) * C1].astype(F32) + up[h * B : h * B + B]
            ox[at : at + B, :] = o.astype(BF)
    send_ref[...] = nn(from_parity(), ox[...]).astype(BF)


def gcoarse_kernel(me, g_ref, hd_ref, hu_ref, cact_ref, wc, m0, m1, m2, m3, back_ref, gv):
    gv[B : 3 * B, C2 : 2 * C2] = g_ref[...]
    for s, ref in ((slice(0, B), hd_ref), (slice(3 * B, 4 * B), hu_ref)):
        gv[s, C2 : C2 + C1] = ref[384:448, :]
        gv[s, C2 + C1 : 2 * C2] = ref[448:512, :]
    for h in range(4):
        s = slice(h * B, h * B + B)
        gf = gv[s, C2 : 2 * C2].astype(F32)
        gv[s, 0:C2] = next_col(gf).astype(BF)
        gv[s, 2 * C2 : 3 * C2] = prev_col(gf).astype(BF)
    q = iota((C2, 160), 1)
    core = jnp.where(q >= 80, 1, 0)
    hi = jnp.where(q - 80 * core >= 40, 1, 0)
    channel = (hi * 8 + core) * 40 + q - 80 * core - 40 * hi
    for n, ref in enumerate((m0, m1, m2, m3)):
        pick = one_hot(iota((C2, 160), 0) == channel + lax.rem(me[3] + n, 4) * 80)
        part = nn(gv[:, C2 : 2 * C2], pick).astype(BF)
        ref[:, 0:C2] = cact_ref[...]
        ref[:, C2 : C2 + 160] = part[0:128]
        ref[:, C2 + 160 : C2 + 320] = part[128:256]
    back = None
    for i in (2, 1, 0):
        t = nn(gv[(2 - i) * B : (2 - i) * B + 128, :], wc[i])
        back = t if back is None else back + t
    back_ref[...] = back


def gresid_kernel(cot_ref, g_ref, back_ref, low_ref, wd, gres_ref, geo_ref, glow_ref, up_ref, down_ref):
    glow = g_ref[...].astype(F32) + back_ref[...] * silu_grad(low_ref[...].astype(F32))
    glow = glow.astype(BF)
    glow_ref[...] = glow
    for k in range(4):
        spread = nn(glow, wd[k])
        par = k % 2
        for h in range(2):
            row = 2 * h + k // 2
            s = slice(row * 128 + par * B, row * 128 + par * B + B)
            c = cot_ref[h * B : h * B + B, k * C1 : (k + 1) * C1].astype(F32)
            grb = (c + spread[h * B : h * B + B]).astype(BF)
            gres_ref[s, :] = grb
            geo_ref[par * 256 + row * B : par * 256 + row * B + B, :] = grb
            if row == 0:
                up_ref[par * B : par * B + B, :] = grb
            if row == 3:
                down_ref[par * B : par * B + B, :] = grb


def gnorm_kernel(x_ref, st_ref, geo, hd_ref, hu_ref, wf, gn_ref, st2_ref, rv):
    for row in range(-1, 5):
        to = slice((row + 1) * B, (row + 2) * B)
        for par in range(2):
            ref, at = (hd_ref, 0) if row < 0 else (hu_ref, 0) if row > 3 else (geo, row * B)
            at += par * (256 if 0 <= row < 4 else B)
            grb = ref[at : at + B, :]
            gr = grb.astype(F32)
            rv[1 + par, to, :] = grb
            if par == 0:
                rv[3, to, :] = next_col(gr).astype(BF)
            else:
                rv[0, to, :] = prev_col(gr).astype(BF)
    mean, rstd = norm_of(st_ref)
    s1 = jnp.zeros((1, C1), F32)
    s2 = jnp.zeros((1, C1), F32)
    for par in range(2):
        acc = None
        for i in range(3):
            for j in range(3):
                t = nt(rv[par + 2 - j, (2 - i) * B : (2 - i) * B + 256, :], wf[3 * i + j])
                acc = t if acc is None else acc + t
        for row in range(4):
            s = slice(row * 128 + par * B, row * 128 + par * B + B)
            z = (x_ref[s, :].astype(F32) - mean) * rstd
            gn = acc[row * B : row * B + B] * silu_grad(z)
            gn_ref[s, :] = gn
            s1 = s1 + jnp.sum(gn, axis=0, keepdims=True)
            s2 = s2 + jnp.sum(gn * z, axis=0, keepdims=True)
    st2_ref[...] = rows8(s1, s2)


def grad_latent_kernel(x_ref, st_ref, gn_ref, gres_ref, st2_ref, send_ref, out_ref, token):
    token[...] = jnp.zeros((8, 128), F32)
    mean, rstd = norm_of(st_ref)
    m = group_sums(st2_ref[...]) / COUNT
    z = (x_ref[...].astype(F32) - mean) * rstd
    g = gres_ref[...].astype(F32) + rstd * (gn_ref[...] - m[0:1] - z * m[1:2])
    g = nn(from_parity(), g.astype(BF)).astype(BF)
    for f in range(16):
        out_ref[f, 0:32, :] = send_ref[32 * f : 32 * f + 32, :]
        out_ref[f, 32:64, :] = g[32 * f : 32 * f + 32]


def places(me, rows):
    q = iota((C2, rows), 0)
    core = jnp.where(q >= C1, 1, 0)
    rest = q - C1 * core
    block = (rest * 1639) >> 16
    return ((block & 1) ^ me[5]) * 8 + (block >> 1) * 2 + core, rest - 40 * block


def turn_grads_kernel(me, geo, cot, glow, gt, ct, lt):
    c = iota((C2, C1), 1)
    block, rest = places(me, C1)
    fine = one_hot((rest < 20) & (c == block * 20 + rest))
    up = one_hot((rest >= 20) & (c == block * 20 + rest - 20))
    gt[...] = nt(fine, geo[...]).astype(BF)
    for k in range(4):
        ct[k] = nt(up, cot[:, k * C1 : (k + 1) * C1]).astype(BF)
    block, rest = places(me, C2)
    lt[...] = nt(one_hot(iota((C2, C2), 1) == block * 40 + rest), glow[...]).astype(BF)


def weight_kernel(me, gt, ct, lt, ave, avo, coarse, depth, keep, send, acc):
    for slot, ref in ((0, keep), (1, send)):
        rows = pl.ds(pl.multiple_of((me[2] ^ slot) * C1, 64), C1)
        for i in range(3):
            s = slice(i * B, i * B + 256)
            both = jnp.concatenate([ave[s, :], avo[s, :]], axis=0)
            acc[:, i * 960 : (i + 1) * 960] = nn(gt[rows, :], both)
        for k in range(4):
            s = slice(k * C2, (k + 1) * C2)
            ref[:, s] = (acc[:, s] + nn(ct[k, rows, :], coarse[...])).astype(BF)
        ref[:, 2560:2880] = acc[:, 2560:2880].astype(BF)
        ref[:, 2880:2944] = jnp.zeros((C1, 64), BF)
        ref[:, 2944:4224] = nn(lt[rows, :], depth[...]).astype(BF)


def coarse_kernel(me, m0, m1, m2, m3, keep, send, a, res):
    eye = one_hot(iota((160, 160), 0) == iota((160, 160), 1))
    lane = iota((160, 256), 1) & 63
    for s, ref in enumerate((m0, m1, m2, m3)):
        f = nt(eye, jnp.concatenate([ref[:, C2 : C2 + 160], ref[:, C2 + 160 : C2 + 320]], axis=0))
        taps = (
            jnp.where(lane == 63, 0.0, pltpu.roll(f, 255, 1)),
            f,
            jnp.where(lane == 0, 0.0, pltpu.roll(f, 1, 1)),
        )
        at = slice(s * 128, s * 128 + 128)
        for j, v in enumerate(taps):
            mid = pltpu.roll(v, 192, 1)
            a[j * 160 : j * 160 + 160, at] = v[:, 128:256].astype(BF)
            a[(3 + j) * 160 : (3 + j) * 160 + 160, at] = mid[:, 0:128].astype(BF)
            a[(6 + j) * 160 : (6 + j) * 160 + 160, at] = v[:, 0:128].astype(BF)
    act = jnp.concatenate([m0[:, 0:C2], m1[:, 0:C2], m2[:, 0:C2], m3[:, 0:C2]], axis=0)
    res[...] = nn(a[...], act)
    for slot, ref in ((0, keep), (1, send)):
        for t in range(9):
            for e in range(2):
                at = t * 160 + (me[2] ^ slot) * 80 + (me[5] ^ e) * 40
                v = res[pl.ds(pl.multiple_of(at, 8), 40), :].astype(BF)
                for i in range(8):
                    to = lax.rem(i // 2 + 4 - me[0], 4) * 4 + ((i % 2) ^ me[1]) * 2 + e
                    ref[to, :, t * 80 : t * 80 + 80] = v[:, i * 80 : i * 80 + 80]


def pack_kernel(me, a_ref, o0, o1, o2, o3, acc, low, high, out):
    acc[...] = (a_ref[0].astype(F32) + a_ref[1].astype(F32)) + (a_ref[2].astype(F32) + a_ref[3].astype(F32))
    low[...] = jnp.zeros(low.shape, F32)
    high[...] = jnp.zeros(high.shape, F32)
    row = iota((80, 384), 0)
    first = jnp.where(row >= 40, row - 40, row) < 20
    for i in range(8):
        for t in range(9):
            low[:, t * 40 : t * 40 + 40] = acc[:, t * C1 + i * 40 : t * C1 + i * 40 + 40]
        for k in range(4):
            high[:, k * 80 : k * 80 + 80] = acc[:, k * C2 + i * 80 : k * C2 + i * 80 + 80]
        to = lax.rem(i // 2 + 4 - me[0], 4) * 2 + ((i % 2) ^ me[1])
        out[to, :, 0:384] = jnp.where(first, low[:, 0:384], high[:, 0:384]).astype(BF)
        for k in range(4):
            at = 2944 + k * C1 + i * 40
            high[:, 384 + k * 40 : 424 + k * 40] = acc[:, at : at + 40]
        out[to, :, 384:640] = high[:, 384:640].astype(BF)
    for n, ref in enumerate((o0, o1, o2, o3)):
        ref[...] = out[2 * n : 2 * n + 2]


def join_kernel(a, b, c, d, coarse, *outs):
    for n, ref in enumerate(outs):
        s = slice(n % 2 * 40, n % 2 * 40 + 40)
        total = a[n // 2, s, :].astype(F32) + b[n // 2, s, :].astype(F32)
        total = total + c[n // 2, s, :].astype(F32) + d[n // 2, s, :].astype(F32)
        ref[:, 0:C2] = total.astype(BF)
        ref[:, C2:] = coarse[n]


def finish_kernel(scale, a_ref, b_ref, c_ref, d_ref, fine_ref, down_ref, coarse_ref, up_ref, u):
    total = a_ref[...].astype(F32) + b_ref[...].astype(F32)
    total = (total + c_ref[...].astype(F32) + d_ref[...].astype(F32)) * scale
    for t in range(9):
        fine_ref[t] = total[0:20, t * 40 : t * 40 + 40]
    u[...] = jnp.zeros(u.shape, F32)
    for k in range(4):
        up_ref[:, k, :] = total[20:40, k * 80 : k * 80 + 80]
        u[0:40, 0:40] = total[:, 384 + k * 40 : 424 + k * 40]
        down_ref[k] = jnp.transpose(u[...])[0:40, 0:40]
    for t in range(9):
        coarse_ref[t] = total[:, C2 + t * 80 : C2 + t * 80 + 80]


def pair_kernel(mine, got, *outs):
    for n, ref in enumerate(outs):
        s = slice(4 * n, 4 * n + 4)
        ref[...] = (mine[s].astype(F32) + got[s].astype(F32)).astype(BF)


def slab_kernel(mine, got, st, out_ref, st_ref):
    st_ref[...] = st[...]
    for n in range(8):
        out_ref[n] = (mine[n].astype(F32) + got[n].astype(F32)).astype(BF)


def add(*terms):
    total = terms[0].astype(F32)
    for t in terms[1:]:
        total = total + t.astype(F32)
    return total.astype(BF)


def other_core(v):
    return lax.ppermute(v, "wa", [(w, w ^ 1) for w in range(16)])


def ring_x(v, step):
    return lax.ppermute(v, "ha", [(h, ((h // 2 + step) % 4) * 2 + h % 2) for h in range(8)])


def other_y(v):
    return lax.ppermute(v, "ha", [(h, h ^ 1) for h in range(8)])


def ring_z(v, step):
    return lax.ppermute(
        v, "wa", [(w, (w // 8) * 8 + ((w // 2 + step) % 4) * 2 + w % 2) for w in range(16)]
    )


def other_y_hi(v):
    return lax.ppermute(v, "wa", [(w, w ^ 8) for w in range(16)])


def to_next(v):
    return lax.ppermute(v, "ha", [(h, h + 1) for h in range(7)])


def to_prev(v):
    return lax.ppermute(v, "ha", [(h + 1, h) for h in range(7)])


def swap_wa(v):
    return lax.all_to_all(v, "wa", 0, 0, tiled=True)


def other_both(v):
    pairs = [(h * 16 + w, (h ^ 1) * 16 + (w ^ 8)) for h in range(8) for w in range(16)]
    return lax.ppermute(v, ("ha", "wa"), pairs)


def swap_z(v):
    groups = [[hi * 8 + z * 2 + core for z in range(4)] for hi in range(2) for core in range(2)]
    return lax.all_to_all(v, "wa", 0, 0, axis_index_groups=groups, tiled=True)


def shards(latent, cotangent, w_fine, w_down, w_coarse, w_up):
    ha, wa = (lax.axis_index("ha"), lax.axis_index("wa"))
    edge = jnp.stack([ha == 0, ha == 7]).astype(jnp.int32)
    me = jnp.stack([ha // 2, ha % 2, wa % 2, (wa // 2) % 4, wa, wa // 8]).astype(jnp.int32)
    frames, rows, cols, _ = latent.shape
    scale = float(frames * 32 * 128) ** (-0.5)
    up_t = jnp.swapaxes(w_up, 1, 2)

    lat = latent.reshape(16, 32, C1)
    both = swap_wa(jnp.concatenate([lat, cotangent.reshape(16, 32, C1)], axis=1))
    wct, token = turned([w_coarse], 9)
    x, up, down, cotk, g, st = call(
        sort_kernel,
        [
            sds((512, C1)),
            sds((512, C1)),
            sds((512, C1)),
            sds((128, 4 * C1)),
            sds((128, C2)),
            sds((8, C1), F32),
        ],
        2,
        us=4,
        after=(token,),
    )(both.reshape(1024, C1), up_t.reshape(4 * C1, C2))
    st_y = st + other_y(st)
    st = st_y + ring_x(st_y, 1) + ring_x(st_y, 2) + ring_x(st_y, 3)
    hd, hu = (to_next(down), to_prev(up))

    wdt, wun, _ = turned([w_down, up_t], 4, after=(st_y,))
    ave, avo, low, cact, depth, cv = call(
        forward_kernel,
        [
            sds((384, 3 * C1)),
            sds((384, 3 * C1)),
            sds((128, C2)),
            sds((128, C2)),
            sds((128, 4 * C1)),
            sds((256, 3 * C2)),
        ],
        6,
        [pltpu.VMEM((640, 3 * C1), BF), pltpu.VMEM((640, 3 * C1), BF), pltpu.VMEM((256, 4 * C1), BF)],
        smem=1,
        us=7,
    )(edge, x, hd, hu, st, w_fine.reshape(3, 3 * C1, C1), w_down.reshape(4 * C1, C2))
    send, coarse = call(
        coarse_level_kernel,
        [sds((512, C1)), sds((128, C2))],
        5,
        [pltpu.VMEM((512, C1), BF)],
        us=3,
    )(cv, low, depth, w_coarse.reshape(3, 3 * C2, C2), wun)

    m0, m1, m2, m3, back = call(
        gcoarse_kernel,
        [sds((128, 960))] * 4 + [sds((128, C2), F32)],
        5,
        [pltpu.VMEM((256, 3 * C2), BF)],
        smem=1,
        us=6,
    )(me, g, hd, hu, cact, wct.reshape(3, 3 * C2, C2))
    m1, m2, m3 = (ring_z(v, n + 1) for n, v in enumerate((m1, m2, m3)))

    gres, geo, glow, up, down = call(
        gresid_kernel,
        [sds((512, C1)), sds((512, C1)), sds((128, C2)), sds((128, C1)), sds((128, C1))],
        5,
        us=3,
    )(cotk, g, back, low, wdt)
    ed, eu = (to_next(down), to_prev(up))

    gt, ct, lt = call(
        turn_grads_kernel,
        [sds((C2, 512)), sds((4, C2, 128)), sds((C2, 128))],
        3,
        smem=1,
        us=3,
        after=(m1[:8, :128] + m2[:8, :128] + m3[:8, :128],),
    )(me, geo, cotk, glow)
    kw, sw = call(
        weight_kernel,
        [sds((C1, 4224))] * 2,
        7,
        [pltpu.VMEM((C1, 2880), F32)],
        smem=1,
        us=7,
        after=(ed, eu),
    )(me, gt, ct, lt, ave, avo, coarse, depth)
    got_w = other_core(sw)
    gn, st2 = call(
        gnorm_kernel,
        [sds((512, C1), F32), sds((8, C1), F32)],
        6,
        [pltpu.VMEM((4, 384, C1), BF)],
        us=6,
        after=(sw,),
    )(x, st, geo, ed, eu, w_fine)
    pair_w, st2 = call(slab_kernel, [sds((8, 40, 4224)), sds((8, C1), F32)], 3, us=4)(
        kw.reshape(8, 40, 4224), got_w.reshape(8, 40, 4224), st2
    )
    sums_w = swap_z(pair_w.reshape(4, 80, 4224))
    st2_y = st2 + other_y(st2)
    st2 = st2_y + ring_x(st2_y, 1) + ring_x(st2_y, 2) + ring_x(st2_y, 3)
    kc, sc = call(
        coarse_kernel,
        [sds((16, 40, 720))] * 2,
        4,
        [pltpu.VMEM((1440, 512), BF), pltpu.VMEM((1440, C2), F32)],
        smem=1,
        us=1,
        after=(st2_y,),
    )(me, m0, m1, m2, m3)
    got_c = other_core(sc)

    pair_c = call(pair_kernel, [sds((4, 40, 720))] * 4, 2, us=1, after=(st2_y,))(kc, got_c)
    coarse_x = add(pair_c[0], *[ring_x(pair_c[n], n) for n in range(1, 4)])

    gsend, token = call(grad_latent_kernel, [sds((16, 64, C1)), sds((8, 128), F32)], 6, us=1, after=(coarse_x[0, :8, :128],))(
        x, st, gn, gres, st2, send
    )
    home = swap_wa(gsend)
    output = home[:, :32].reshape(frames, rows, cols, C1)
    grad_latent = home[:, 32:].reshape(frames, rows, cols, C1)

    packed = call(
        pack_kernel,
        [sds((2, 80, C2))] * 4,
        1,
        [
            pltpu.VMEM((80, 4224), F32),
            pltpu.VMEM((80, C2), F32),
            pltpu.VMEM((80, C2), F32),
            pltpu.VMEM((8, 80, C2), BF),
        ],
        smem=1,
        us=0,
        after=(coarse_x, token),
    )(me, sums_w)
    joined = call(join_kernel, [sds((40, 1360))] * 4, 5, us=0, after=(home[0, :8, :128],))(
        packed[0], *[ring_x(packed[n], n) for n in range(1, 4)], coarse_x
    )
    fine, down, coarse_w, up = call(
        functools.partial(finish_kernel, scale),
        [sds((9, 20, 40), F32), sds((4, 40, 40), F32), sds((9, 40, 80), F32), sds((20, 4, 80), F32)],
        4,
        [pltpu.VMEM((128, 128), F32)],
    )(joined[0], other_y(joined[2]), other_y_hi(joined[1]), other_both(joined[3]))
    fine, coarse_w = (jnp.swapaxes(v, 1, 2) for v in (fine, coarse_w))
    return output, grad_latent, fine, down, coarse_w, jnp.transpose(up, (1, 2, 0))


def solution(mesh):
    big, small = (P(None, "ha", "wa", None), P(None, "ha", "wa"))
    return jax.shard_map(
        shards,
        mesh=mesh,
        in_specs=(big, big, P(), P(), P(), P()),
        out_specs=(big, big, small, small, small, small),
        check_vma=False,
    )
```

profile of v0, /device:TPU:0, one launch (start us, length us, event | category | flops | bytes accessed | tf_op | source)
XLA Modules:
  0.0 161.6 jit_solution(667676092009059710)
XLA Ops:
  2.8 8.1 %all-to-all-start = ((bf16[16,64,320]{2,1,0:T(8,128)(2,1)}), bf16[16,64,320]{2,1,0:T(8,128)(2,1)S(1)}, u32[]{:S(2)}, u32[]{:S(2)}) async-start(bf16[16,64,320]{2,1,0:T(8,128)(2,1)} %pad_maximum_fusion), calls=%async_computation | async-start | bytes 1572864 | tf_op jit(solution)/shard_map/all_to_all | solution.py:490
  11.0 3.1 %copy-done.6 = bf16[9,640,640]{2,1,0:T(8,128)(2,1)S(1)} copy-done((bf16[9,640,640]{2,1,0:T(8,128)(2,1)S(1)}, bf16[9,640,640]{2,1,0:T(8,128)(2,1)}, u32[]{:S(2)}) %copy-start.6) | copy-done | bytes 7372824
  16.6 2.9 %copy-done.11 = bf16[9,640,640]{2,1,0:T(8,128)(2,1)} copy-done((bf16[9,640,640]{2,1,0:T(8,128)(2,1)}, bf16[9,640,640]{2,1,0:T(8,128)(2,1)S(1)}, u32[]{:S(2)}) %copy-start.11) | copy-done | bytes 7372824
  19.5 6.6 %all-to-all-done = bf16[16,64,320]{2,1,0:T(8,128)(2,1)S(1)} async-done(((bf16[16,64,320]{2,1,0:T(8,128)(2,1)}), bf16[16,64,320]{2,1,0:T(8,128)(2,1)S(1)}, u32[]{:S(2)}, u32[]{:S(2)}) %all-to-all-start) | async-done | bytes 655392 | tf_op jit(solution)/shard_map/all_to_all | solution.py:490
  30.9 3.2 %collective-permute-start.4 = (bf16[512,320]{1,0:T(8,128)(2,1)S(1)}, bf16[512,320]{1,0:T(8,128)(2,1)S(1)}, u32[]{:S(2)}, u32[]{:S(2)}) collective-permute-start(bf16[512,320]{1,0:T(8,128)(2,1)S(1)} %get-tuple-element.68), channel_id=1, source_target_pairs={{0,16},{16,32},{32,48},{48,64},{64,80},{80,96},{96,112},{1,17},{17... | collective-permute-start | bytes 983048 | tf_op jit(solution)/shard_map/ppermute | solution.py:482
  35.5 5.0 %collective-permute-start.3 = (f32[8,320]{1,0:T(8,128)S(1)}, f32[8,320]{1,0:T(8,128)S(1)}, u32[]{:S(2)}, u32[]{:S(2)}) collective-permute-start(f32[8,320]{1,0:T(8,128)S(1)} %add.52.refs_2_), channel_id=1, source_target_pairs={{0,96},{16,112},{32,0},{48,16},{64,32},{80,48},{96,64},{112,80},{1... | collective-permute-start | bytes 30728 | tf_op jit(solution)/shard_map/ppermute | solution.py:464
  47.6 2.8 %collective-permute-done.4.refs_2_ = bf16[512,320]{1,0:T(8,128)(2,1)S(1)} collective-permute-done((bf16[512,320]{1,0:T(8,128)(2,1)S(1)}, bf16[512,320]{1,0:T(8,128)(2,1)S(1)}, u32[]{:S(2)}, u32[]{:S(2)}) %collective-permute-start.4) | collective-permute-done | bytes 327712 | tf_op jit(solution)/shard_map/ppermute | solution.py:482
  50.5 6.1 %shard_map.111 = (bf16[384,960]{1,0:T(8,128)(2,1)S(1)}, bf16[384,960]{1,0:T(8,128)(2,1)S(1)}, bf16[128,640]{1,0:T(8,128)(2,1)S(1)}, bf16[128,640]{1,0:T(8,128)(2...) custom-call(s32[2]{0:T(128)S(1)} %add_convert_fusion.1.refs_0_, bf16[512,320]{1,0:T(8,128)(2,1)S(1)} %copy-done.17, ...), custom_call_target="tpu_custom_call" | custom-call | flops 7000000000 | bytes 1000000 | tf_op jit(solution)/shard_map/pallas_call | solution.py:120
  56.7 2.5 %shard_map.112 = (bf16[128,960]{1,0:T(8,128)(2,1)S(1)}, bf16[128,960]{1,0:T(8,128)(2,1)S(1)}, bf16[128,960]{1,0:T(8,128)(2,1)S(1)}, bf16[128,960]{1,0:T(8,128)(2,1)S(1)}, f32[128,640]{1,0:T(8,128)S(1)}) custom-call(s32[6]{0:T(128)S(1)} %stack.36.refs_0_, bf16[128,640]{1,0:T(8,128)(2,1)S(1)} %copy-done.26, ...), custom_call_target="tpu_custom_call" | custom-call | flops 6000000000 | bytes 1000000 | tf_op jit(solution)/shard_map/pallas_call | solution.py:120
  59.9 3.2 %collective-permute-start.9 = (bf16[128,960]{1,0:T(8,128)(2,1)S(1)}, bf16[128,960]{1,0:T(8,128)(2,1)S(1)}, u32[]{:S(2)}, u32[]{:S(2)}) collective-permute-start(bf16[128,960]{1,0:T(8,128)(2,1)S(1)} %get-tuple-element.80), channel_id=1, source_target_pairs={{0,4},{1,5},{2,6},{3,7},{4,0},{5,1},{6,2},{7,3},{8,12},{9,13},{10,... | collective-permute-start | bytes 737288 | tf_op jit(solution)/shard_map/ppermute | solution.py:472
  64.0 4.4 %collective-permute-start.6 = (bf16[128,320]{1,0:T(8,128)(2,1)S(1)}, bf16[128,320]{1,0:T(8,128)(2,1)S(1)}, u32[]{:S(2)}, u32[]{:S(2)}) collective-permute-start(bf16[128,320]{1,0:T(8,128)(2,1)S(1)} %get-tuple-element.76), channel_id=1, source_target_pairs={{0,16},{16,32},{32,48},{48,64},{64,80},{80,96},{96,112},{1,17},{17... | collective-permute-start | bytes 245768 | tf_op jit(solution)/shard_map/ppermute | solution.py:482
  76.1 4.1 %shard_map.117 = (bf16[320,4224]{1,0:T(8,128)(2,1)S(1)}, bf16[320,4224]{1,0:T(8,128)(2,1)S(1)}) custom-call(s32[6]{0:T(128)S(1)} %stack.36.refs_0_, bf16[640,512]{1,0:T(8,128)(2,1)S(1)} %get-tuple-element.82.refs_1_, bf16[4,640,128]{2,1,0:T(8,128)(2,1)S(1)} %get-tuple-element.83.refs_2_, bf16[640,128]{1,0:T(8,128)(2,1)S(1)} %get-tuple-element.84.refs_3_, ...), custom_call_target="tpu_custom_call" | custom-call | flops 7000000000 | bytes 1000000 | tf_op jit(solution)/shard_map/pallas_call | solution.py:120
  80.3 2.7 %shard_map.118 = (f32[512,320]{1,0:T(8,128)S(1)}, f32[8,320]{1,0:T(8,128)S(1)}) custom-call(bf16[512,320]{1,0:T(8,128)(2,1)S(1)} %copy-done.17, f32[8,320]{1,0:T(8,128)S(1)} %add_add_fusion.1.refs_4_.refs_1_, bf16[512,320]{1,0:T(8,128)(2,1)S(1)} %get-tuple-element.75.refs_1_.refs_2_, bf16[128,320]{1,0:T(8,128)(2,1)S(1)} %collective-permute-done.6.refs_8_.refs_3_, ...), custom_call_target="tpu_custom_call" | custom-call | flops 6000000000 | bytes 1000000 | tf_op jit(solution)/shard_map/pallas_call | solution.py:120
  87.4 3.8 %all-to-all-start.2 = ((bf16[4,80,4224]{2,1,0:T(8,128)(2,1)}), bf16[4,80,4224]{2,1,0:T(8,128)(2,1)S(1)}, u32[]{:S(2)}, u32[]{:S(2)}) async-start(bf16[4,80,4224]{2,1,0:T(8,128)(2,1)} %bitcast.32), calls=%async_computation.2 | async-start | bytes 5406720 | tf_op jit(solution)/shard_map/all_to_all | solution.py:500
  91.2 2.7 %collective-permute-start.12 = (f32[8,320]{1,0:T(8,128)S(1)}, f32[8,320]{1,0:T(8,128)S(1)}, u32[]{:S(2)}, u32[]{:S(2)}) collective-permute-start(f32[8,320]{1,0:T(8,128)S(1)} %get-tuple-element.96), channel_id=1, source_target_pairs={{0,16},{16,0},{32,48},{48,32},{64,80},{80,64},{96,112},{112,96},{1... | collective-permute-start | bytes 30728 | tf_op jit(solution)/shard_map/ppermute | solution.py:468
  98.4 4.1 %shard_map.120 = (bf16[16,40,720]{2,1,0:T(8,128)(2,1)S(1)}, bf16[16,40,720]{2,1,0:T(8,128)(2,1)S(1)}) custom-call(s32[6]{0:T(128)S(1)} %stack.36.refs_0_, bf16[128,960]{1,0:T(8,128)(2,1)S(1)} %copy-done.22, bf16[128,960]{1,0:T(8,128)(2,1)S(1)} %collective-permute-done.8.refs_2_, bf16[128,960]{1,0:T(8,128)(2,1)S(1)} %copy-done.3, ...), custom_call_target="tpu_custom_call" | custom-call | flops 1000000000 | bytes 1000000 | tf_op jit(solution)/shard_map/pallas_call | solution.py:120
  102.6 5.8 %collective-permute-start.15 = (f32[8,320]{1,0:T(8,128)S(1)}, f32[8,320]{1,0:T(8,128)S(1)}, u32[]{:S(2)}, u32[]{:S(2)}) collective-permute-start(f32[8,320]{1,0:T(8,128)S(1)} %add.61.refs_5_.refs_2_), channel_id=1, source_target_pairs={{0,96},{16,112},{32,0},{48,16},{64,32},{80,48},{96,64},{112,80},{1... | collective-permute-start | bytes 30728 | tf_op jit(solution)/shard_map/ppermute | solution.py:464
  115.1 5.2 %collective-permute-done.17 = bf16[4,40,720]{2,1,0:T(8,128)(2,1)S(1)} collective-permute-done((bf16[4,40,720]{2,1,0:T(8,128)(2,1)S(1)}, bf16[4,40,720]{2,1,0:T(8,128)(2,1)S(1)}, u32[]{:S(2)}, u32[]{:S(2)}) %collective-permute-start.17) | collective-permute-done | bytes 230432 | tf_op jit(solution)/shard_map/ppermute | solution.py:464
  120.3 4.7 %collective-permute-done.18 = bf16[4,40,720]{2,1,0:T(8,128)(2,1)S(1)} collective-permute-done((bf16[4,40,720]{2,1,0:T(8,128)(2,1)S(1)}, bf16[4,40,720]{2,1,0:T(8,128)(2,1)S(1)}, u32[]{:S(2)}, u32[]{:S(2)}) %collective-permute-start.18) | collective-permute-done | bytes 230432 | tf_op jit(solution)/shard_map/ppermute | solution.py:464
  127.3 5.5 %all-to-all-start.1 = ((bf16[16,64,320]{2,1,0:T(8,128)(2,1)}), bf16[16,64,320]{2,1,0:T(8,128)(2,1)}, u32[]{:S(2)}, u32[]{:S(2)}) async-start(bf16[16,64,320]{2,1,0:T(8,128)(2,1)} %copy-done.1), calls=%async_computation.1 | async-start | bytes 1572864 | tf_op jit(solution)/shard_map/all_to_all | solution.py:490
  132.8 3.3 %shard_map.123 = (bf16[2,80,640]{2,1,0:T(8,128)(2,1)S(1)}, bf16[2,80,640]{2,1,0:T(8,128)(2,1)}, bf16[2,80,640]{2,1,0:T(8,128)(2,1)}, bf16[2,80,640]{2,1,0:T(8,128)(2,1)S(1)}) custom-call(s32[6]{0:T(128)S(1)} %stack.36.refs_0_, bf16[4,80,4224]{2,1,0:T(8,128)(2,1)S(1)} %all-to-all-done.2.refs_1_, bf16[4,40,720]{2,1,0:T(8,128)(2,1)S(1)} %add_convert_fusion.refs_2_.refs_4_, ...), custom_call_target="tpu_custom_call" | custom-call | bytes 1000000 | tf_op jit(solution)/shard_map/pallas_call | solution.py:120
  137.7 2.5 %collective-permute-start.21 = (bf16[2,80,640]{2,1,0:T(8,128)(2,1)}, bf16[2,80,640]{2,1,0:T(8,128)(2,1)S(1)}, u32[]{:S(2)}, u32[]{:S(2)}) collective-permute-start(bf16[2,80,640]{2,1,0:T(8,128)(2,1)} %get-tuple-element.110), channel_id=1, source_target_pairs={{0,64},{16,80},{32,96},{48,112},{64,0},{80,16},{96,32},{112,48},{1... | collective-permute-start | bytes 614408 | tf_op jit(solution)/shard_map/ppermute | solution.py:464
  141.2 6.8 %all-to-all-done.1 = bf16[16,64,320]{2,1,0:T(8,128)(2,1)} async-done(((bf16[16,64,320]{2,1,0:T(8,128)(2,1)}), bf16[16,64,320]{2,1,0:T(8,128)(2,1)}, u32[]{:S(2)}, u32[]{:S(2)}) %all-to-all-start.1) | async-done | bytes 655392 | tf_op jit(solution)/shard_map/all_to_all | solution.py:490
  150.4 3.3 %collective-permute-start.24 = (bf16[40,1360]{1,0:T(8,128)(2,1)S(1)}, bf16[40,1360]{1,0:T(8,128)(2,1)S(1)}, u32[]{:S(2)}, u32[]{:S(2)}) collective-permute-start(bf16[40,1360]{1,0:T(8,128)(2,1)S(1)} %get-tuple-element.114), channel_id=1, source_target_pairs={{0,8},{1,9},{2,10},{3,11},{4,12},{5,13},{6,14},{7,15},{8,0},{9,1},... | collective-permute-start | bytes 326408 | tf_op jit(solution)/shard_map/ppermute | solution.py:478
  (127 shorter events, 57.8 us)
Async XLA Ops:
  2.8 23.3 %all-to-all-start = ((bf16[16,64,320]{2,1,0:T(8,128)(2,1)}), bf16[16,64,320]{2,1,0:T(8,128)(2,1)S(1)}, u32[]{:S(2)}, u32[]{:S(2)}) async-start(bf16[16,64,320]{2,1,0:T(8,128)(2,1)} %pad_maximum_fusion), calls=%async_computation | async-start | bytes 1572864 | tf_op jit(solution)/shard_map/all_to_all | solution.py:490
  30.9 19.5 %collective-permute-start.4 = (bf16[512,320]{1,0:T(8,128)(2,1)S(1)}, bf16[512,320]{1,0:T(8,128)(2,1)S(1)}, u32[]{:S(2)}, u32[]{:S(2)}) collective-permute-start(bf16[512,320]{1,0:T(8,128)(2,1)S(1)} %get-tuple-element.68), channel_id=1, source_target_pairs={{0,16},{16,32},{32,48},{48,64},{64,80},{80,96},{96,112},{1,17},{17... | collective-permute-start | bytes 983048 | tf_op jit(solution)/shard_map/ppermute | solution.py:482
  34.2 16.3 %collective-permute-start.5 = (bf16[512,320]{1,0:T(8,128)(2,1)S(1)}, bf16[512,320]{1,0:T(8,128)(2,1)S(1)}, u32[]{:S(2)}, u32[]{:S(2)}) collective-permute-start(bf16[512,320]{1,0:T(8,128)(2,1)S(1)} %get-tuple-element.69), channel_id=1, source_target_pairs={{16,0},{32,16},{48,32},{64,48},{80,64},{96,80},{112,96},{17,1},{33... | collective-permute-start | bytes 983048 | tf_op jit(solution)/shard_map/ppermute | solution.py:486
  35.5 12.1 %collective-permute-start.3 = (f32[8,320]{1,0:T(8,128)S(1)}, f32[8,320]{1,0:T(8,128)S(1)}, u32[]{:S(2)}, u32[]{:S(2)}) collective-permute-start(f32[8,320]{1,0:T(8,128)S(1)} %add.52.refs_2_), channel_id=1, source_target_pairs={{0,96},{16,112},{32,0},{48,16},{64,32},{80,48},{96,64},{112,80},{1... | collective-permute-start | bytes 30728 | tf_op jit(solution)/shard_map/ppermute | solution.py:464
  40.5 7.1 %collective-permute-start.2 = (f32[8,320]{1,0:T(8,128)S(1)}, f32[8,320]{1,0:T(8,128)S(1)}, u32[]{:S(2)}, u32[]{:S(2)}) collective-permute-start(f32[8,320]{1,0:T(8,128)S(1)} %add.52.refs_2_), channel_id=1, source_target_pairs={{0,64},{16,80},{32,96},{48,112},{64,0},{80,16},{96,32},{112,48},{1... | collective-permute-start | bytes 30728 | tf_op jit(solution)/shard_map/ppermute | solution.py:464
  59.9 12.2 %collective-permute-start.8 = (bf16[128,960]{1,0:T(8,128)(2,1)S(1)}, bf16[128,960]{1,0:T(8,128)(2,1)S(1)}, u32[]{:S(2)}, u32[]{:S(2)}) collective-permute-start(bf16[128,960]{1,0:T(8,128)(2,1)S(1)} %get-tuple-element.79), channel_id=1, source_target_pairs={{0,2},{1,3},{2,4},{3,5},{4,6},{5,7},{6,0},{7,1},{8,10},{9,11},{10,... | collective-permute-start | bytes 737288 | tf_op jit(solution)/shard_map/ppermute | solution.py:472
  59.9 14.2 %collective-permute-start.9 = (bf16[128,960]{1,0:T(8,128)(2,1)S(1)}, bf16[128,960]{1,0:T(8,128)(2,1)S(1)}, u32[]{:S(2)}, u32[]{:S(2)}) collective-permute-start(bf16[128,960]{1,0:T(8,128)(2,1)S(1)} %get-tuple-element.80), channel_id=1, source_target_pairs={{0,4},{1,5},{2,6},{3,7},{4,0},{5,1},{6,2},{7,3},{8,12},{9,13},{10,... | collective-permute-start | bytes 737288 | tf_op jit(solution)/shard_map/ppermute | solution.py:472
  63.1 11.0 %collective-permute-start.10 = (bf16[128,960]{1,0:T(8,128)(2,1)S(1)}, bf16[128,960]{1,0:T(8,128)(2,1)S(1)}, u32[]{:S(2)}, u32[]{:S(2)}) collective-permute-start(bf16[128,960]{1,0:T(8,128)(2,1)S(1)} %get-tuple-element.81), channel_id=1, source_target_pairs={{0,6},{1,7},{2,0},{3,1},{4,2},{5,3},{6,4},{7,5},{8,14},{9,15},{10,... | collective-permute-start | bytes 737288 | tf_op jit(solution)/shard_map/ppermute | solution.py:472
  64.0 12.1 %collective-permute-start.6 = (bf16[128,320]{1,0:T(8,128)(2,1)S(1)}, bf16[128,320]{1,0:T(8,128)(2,1)S(1)}, u32[]{:S(2)}, u32[]{:S(2)}) collective-permute-start(bf16[128,320]{1,0:T(8,128)(2,1)S(1)} %get-tuple-element.76), channel_id=1, source_target_pairs={{0,16},{16,32},{32,48},{48,64},{64,80},{80,96},{96,112},{1,17},{17... | collective-permute-start | bytes 245768 | tf_op jit(solution)/shard_map/ppermute | solution.py:482
  68.4 7.7 %collective-permute-start.7 = (bf16[128,320]{1,0:T(8,128)(2,1)S(1)}, bf16[128,320]{1,0:T(8,128)(2,1)S(1)}, u32[]{:S(2)}, u32[]{:S(2)}) collective-permute-start(bf16[128,320]{1,0:T(8,128)(2,1)S(1)} %get-tuple-element.77), channel_id=1, source_target_pairs={{16,0},{32,16},{48,32},{64,48},{80,64},{96,80},{112,96},{17,1},{33... | collective-permute-start | bytes 245768 | tf_op jit(solution)/shard_map/ppermute | solution.py:486
  87.4 39.9 %all-to-all-start.2 = ((bf16[4,80,4224]{2,1,0:T(8,128)(2,1)}), bf16[4,80,4224]{2,1,0:T(8,128)(2,1)S(1)}, u32[]{:S(2)}, u32[]{:S(2)}) async-start(bf16[4,80,4224]{2,1,0:T(8,128)(2,1)} %bitcast.32), calls=%async_computation.2 | async-start | bytes 5406720 | tf_op jit(solution)/shard_map/all_to_all | solution.py:500
  102.5 7.6 %collective-permute-start.16 = (bf16[16,40,720]{2,1,0:T(8,128)(2,1)S(1)}, bf16[16,40,720]{2,1,0:T(8,128)(2,1)S(1)}, u32[]{:S(2)}, u32[]{:S(2)}) collective-permute-start(bf16[16,40,720]{2,1,0:T(8,128)(2,1)S(1)} %get-tuple-element.100), channel_id=1, source_target_pairs={{0,1},{1,0},{2,3},{3,2},{4,5},{5,4},{6,7},{7,6},{8,9},{9,8},{10,11... | collective-permute-start | bytes 2764808 | tf_op jit(solution)/shard_map/ppermute | solution.py:460
  102.6 11.7 %collective-permute-start.15 = (f32[8,320]{1,0:T(8,128)S(1)}, f32[8,320]{1,0:T(8,128)S(1)}, u32[]{:S(2)}, u32[]{:S(2)}) collective-permute-start(f32[8,320]{1,0:T(8,128)S(1)} %add.61.refs_5_.refs_2_), channel_id=1, source_target_pairs={{0,96},{16,112},{32,0},{48,16},{64,32},{80,48},{96,64},{112,80},{1... | collective-permute-start | bytes 30728 | tf_op jit(solution)/shard_map/ppermute | solution.py:464
  108.5 6.6 %collective-permute-start.14 = (f32[8,320]{1,0:T(8,128)S(1)}, f32[8,320]{1,0:T(8,128)S(1)}, u32[]{:S(2)}, u32[]{:S(2)}) collective-permute-start(f32[8,320]{1,0:T(8,128)S(1)} %add.61.refs_5_.refs_2_), channel_id=1, source_target_pairs={{0,64},{16,80},{32,96},{48,112},{64,0},{80,16},{96,32},{112,48},{1... | collective-permute-start | bytes 30728 | tf_op jit(solution)/shard_map/ppermute | solution.py:464
  110.4 9.8 %collective-permute-start.17 = (bf16[4,40,720]{2,1,0:T(8,128)(2,1)S(1)}, bf16[4,40,720]{2,1,0:T(8,128)(2,1)S(1)}, u32[]{:S(2)}, u32[]{:S(2)}) collective-permute-start(bf16[4,40,720]{2,1,0:T(8,128)(2,1)S(1)} %get-tuple-element.102), channel_id=1, source_target_pairs={{0,32},{16,48},{32,64},{48,80},{64,96},{80,112},{96,0},{112,16},{1... | collective-permute-start | bytes 691208 | tf_op jit(solution)/shard_map/ppermute | solution.py:464
  112.3 12.7 %collective-permute-start.18 = (bf16[4,40,720]{2,1,0:T(8,128)(2,1)S(1)}, bf16[4,40,720]{2,1,0:T(8,128)(2,1)S(1)}, u32[]{:S(2)}, u32[]{:S(2)}) collective-permute-start(bf16[4,40,720]{2,1,0:T(8,128)(2,1)S(1)} %get-tuple-element.103), channel_id=1, source_target_pairs={{0,64},{16,80},{32,96},{48,112},{64,0},{80,16},{96,32},{112,48},{1... | collective-permute-start | bytes 691208 | tf_op jit(solution)/shard_map/ppermute | solution.py:464
  114.3 10.7 %collective-permute-start.19 = (bf16[4,40,720]{2,1,0:T(8,128)(2,1)S(1)}, bf16[4,40,720]{2,1,0:T(8,128)(2,1)S(1)}, u32[]{:S(2)}, u32[]{:S(2)}) collective-permute-start(bf16[4,40,720]{2,1,0:T(8,128)(2,1)S(1)} %get-tuple-element.104), channel_id=1, source_target_pairs={{0,96},{16,112},{32,0},{48,16},{64,32},{80,48},{96,64},{112,80},{1... | collective-permute-start | bytes 691208 | tf_op jit(solution)/shard_map/ppermute | solution.py:464
  127.3 20.7 %all-to-all-start.1 = ((bf16[16,64,320]{2,1,0:T(8,128)(2,1)}), bf16[16,64,320]{2,1,0:T(8,128)(2,1)}, u32[]{:S(2)}, u32[]{:S(2)}) async-start(bf16[16,64,320]{2,1,0:T(8,128)(2,1)} %copy-done.1), calls=%async_computation.1 | async-start | bytes 1572864 | tf_op jit(solution)/shard_map/all_to_all | solution.py:490
  136.1 12.6 %collective-permute-start.20 = (bf16[2,80,640]{2,1,0:T(8,128)(2,1)}, bf16[2,80,640]{2,1,0:T(8,128)(2,1)S(1)}, u32[]{:S(2)}, u32[]{:S(2)}) collective-permute-start(bf16[2,80,640]{2,1,0:T(8,128)(2,1)} %get-tuple-element.109), channel_id=1, source_target_pairs={{0,32},{16,48},{32,64},{48,80},{64,96},{80,112},{96,0},{112,16},{1... | collective-permute-start | bytes 614408 | tf_op jit(solution)/shard_map/ppermute | solution.py:464
  137.7 12.4 %collective-permute-start.21 = (bf16[2,80,640]{2,1,0:T(8,128)(2,1)}, bf16[2,80,640]{2,1,0:T(8,128)(2,1)S(1)}, u32[]{:S(2)}, u32[]{:S(2)}) collective-permute-start(bf16[2,80,640]{2,1,0:T(8,128)(2,1)} %get-tuple-element.110), channel_id=1, source_target_pairs={{0,64},{16,80},{32,96},{48,112},{64,0},{80,16},{96,32},{112,48},{1... | collective-permute-start | bytes 614408 | tf_op jit(solution)/shard_map/ppermute | solution.py:464
  140.2 9.9 %collective-permute-start.22 = (bf16[2,80,640]{2,1,0:T(8,128)(2,1)S(1)}, bf16[2,80,640]{2,1,0:T(8,128)(2,1)S(1)}, u32[]{:S(2)}, u32[]{:S(2)}) collective-permute-start(bf16[2,80,640]{2,1,0:T(8,128)(2,1)S(1)} %get-tuple-element.111), channel_id=1, source_target_pairs={{0,96},{16,112},{32,0},{48,16},{64,32},{80,48},{96,64},{112,80},{1... | collective-permute-start | bytes 614408 | tf_op jit(solution)/shard_map/ppermute | solution.py:464
  150.3 6.9 %collective-permute-start.23 = (bf16[40,1360]{1,0:T(8,128)(2,1)S(1)}, bf16[40,1360]{1,0:T(8,128)(2,1)S(1)}, u32[]{:S(2)}, u32[]{:S(2)}) collective-permute-start(bf16[40,1360]{1,0:T(8,128)(2,1)S(1)} %get-tuple-element.113), channel_id=1, source_target_pairs={{0,16},{16,0},{32,48},{48,32},{64,80},{80,64},{96,112},{112,96},{1... | collective-permute-start | bytes 326408 | tf_op jit(solution)/shard_map/ppermute | solution.py:468
  150.4 8.3 %collective-permute-start.24 = (bf16[40,1360]{1,0:T(8,128)(2,1)S(1)}, bf16[40,1360]{1,0:T(8,128)(2,1)S(1)}, u32[]{:S(2)}, u32[]{:S(2)}) collective-permute-start(bf16[40,1360]{1,0:T(8,128)(2,1)S(1)} %get-tuple-element.114), channel_id=1, source_target_pairs={{0,8},{1,9},{2,10},{3,11},{4,12},{5,13},{6,14},{7,15},{8,0},{9,1},... | collective-permute-start | bytes 326408 | tf_op jit(solution)/shard_map/ppermute | solution.py:478
  153.6 6.8 %collective-permute-start.25 = (bf16[40,1360]{1,0:T(8,128)(2,1)S(1)}, bf16[40,1360]{1,0:T(8,128)(2,1)S(1)}, u32[]{:S(2)}, u32[]{:S(2)}) collective-permute-start(bf16[40,1360]{1,0:T(8,128)(2,1)S(1)} %get-tuple-element.115), channel_id=1, source_target_pairs={{0,24},{1,25},{2,26},{3,27},{4,28},{5,29},{6,30},{7,31},{8,16},{9,... | collective-permute-start | bytes 326408 | tf_op jit(solution)/shard_map/ppermute | solution.py:495
  (36 other events, 216.0 us)
where the time goes:
time: 163 us; the launch traced here: 162 us
  starting transfers between devices  63.2 us (39%)
  waiting for transfers between devices  38.2 us (23%)
  Pallas kernels  37.3 us (23%)
  local copies, waits for them, and re-layouts  19.3 us (12%)
  other arithmetic  2.44 us (1%)
    pallas_call x15, Pallas kernels, call(): return lambda *args: f(*args, *after)  33 us
    ppermute x12, starting transfers between devices, ring_x(): lax.ppermute(v, 'ha', [(h, (h // 2 + step) % 4 * 2 + h % 2) for h in rang...  24 us
    unnamed x62, local copies, waits for them, and re-layouts  16.5 us
    all_to_all x2, starting transfers between devices, swap_wa(): return lax.all_to_all(v, 'wa', 0, 0, tiled=True)  13.6 us
    ppermute x12, waiting for transfers between devices, ring_x(): lax.ppermute(v, 'ha', [(h, (h // 2 + step) % 4 * 2 + h % 2) for h in rang...  13.6 us
    all_to_all x2, waiting for transfers between devices, swap_wa(): return lax.all_to_all(v, 'wa', 0, 0, tiled=True)  13.4 us
    ppermute x2, starting transfers between devices, to_next(): return lax.ppermute(v, 'ha', [(h, h + 1) for h in range(7)])  7.61 us
    pallas_call x2, Pallas kernels, turned(): pl.pallas_call(functools.partial(turn_kernel, len(weights)), grid=(weight...  4.31 us
  transfers between devices with their start and end apart: 29, of which 12 were waited for; matrix products, arithmetic and copies ran while one was open for 2% of the time, Pallas kernels for 13%

commit v1 on v0

--- a/solution.py
+++ b/solution.py
@@ -601,8 +601,6 @@
         kw.reshape(8, 40, 4224), got_w.reshape(8, 40, 4224), st2
     )
     sums_w = swap_z(pair_w.reshape(4, 80, 4224))
-    st2_y = st2 + other_y(st2)
-    st2 = st2_y + ring_x(st2_y, 1) + ring_x(st2_y, 2) + ring_x(st2_y, 3)
     kc, sc = call(
         coarse_kernel,
         [sds((16, 40, 720))] * 2,
@@ -610,8 +608,10 @@
         [pltpu.VMEM((1440, 512), BF), pltpu.VMEM((1440, C2), F32)],
         smem=1,
         us=1,
-        after=(st2_y,),
+        after=(st2,),
     )(me, m0, m1, m2, m3)
+    st2_y = st2 + other_y(st2)
+    st2 = st2_y + ring_x(st2_y, 1) + ring_x(st2_y, 2) + ring_x(st2_y, 3)
     got_c = other_core(sc)
 
     pair_c = call(pair_kernel, [sds((4, 40, 720))] * 4, 2, us=1, after=(st2_y,))(kc, got_c)

time: 163 us -> 162 us (level)
  no operation moved by 1% of the time
where the time goes in v1:
time: 162 us; the launch traced here: 161 us
  starting transfers between devices  63.9 us (39%)
  Pallas kernels  37.3 us (23%)
  waiting for transfers between devices  36.9 us (23%)
  local copies, waits for them, and re-layouts  19.3 us (12%)
  other arithmetic  2.43 us (2%)
    pallas_call x15, Pallas kernels, call(): return lambda *args: f(*args, *after)  33 us
    ppermute x12, starting transfers between devices, ring_x(): lax.ppermute(v, 'ha', [(h, (h // 2 + step) % 4 * 2 + h % 2) for h in rang...  24.7 us
    unnamed x62, local copies, waits for them, and re-layouts  16.5 us
    all_to_all x2, starting transfers between devices, swap_wa(): return lax.all_to_all(v, 'wa', 0, 0, tiled=True)  13.6 us
    ppermute x12, waiting for transfers between devices, ring_x(): lax.ppermute(v, 'ha', [(h, (h // 2 + step) % 4 * 2 + h % 2) for h in rang...  13 us
    all_to_all x2, waiting for transfers between devices, swap_wa(): return lax.all_to_all(v, 'wa', 0, 0, tiled=True)  12.7 us
    ppermute x2, starting transfers between devices, to_next(): return lax.ppermute(v, 'ha', [(h, h + 1) for h in range(7)])  7.61 us
    pallas_call x2, Pallas kernels, turned(): pl.pallas_call(functools.partial(turn_kernel, len(weights)), grid=(weight...  4.31 us
  transfers between devices with their start and end apart: 29, of which 12 were waited for; matrix products, arithmetic and copies ran while one was open for 2% of the time, Pallas kernels for 13%

profile of v1, /device:TPU:0, one launch (start us, length us, event | category | flops | bytes accessed | tf_op | source)
XLA Modules:
  0.0 161.0 jit_solution(16018311659310781091)
XLA Ops:
  2.8 8.1 %all-to-all-start = ((bf16[16,64,320]{2,1,0:T(8,128)(2,1)}), bf16[16,64,320]{2,1,0:T(8,128)(2,1)S(1)}, u32[]{:S(2)}, u32[]{:S(2)}) async-start(bf16[16,64,320]{2,1,0:T(8,128)(2,1)} %pad_maximum_fusion), calls=%async_computation | async-start | bytes 1572864 | tf_op jit(solution)/shard_map/all_to_all | solution.py:490
  11.0 3.1 %copy-done.6 = bf16[9,640,640]{2,1,0:T(8,128)(2,1)S(1)} copy-done((bf16[9,640,640]{2,1,0:T(8,128)(2,1)S(1)}, bf16[9,640,640]{2,1,0:T(8,128)(2,1)}, u32[]{:S(2)}) %copy-start.6) | copy-done | bytes 7372824
  16.6 2.9 %copy-done.11 = bf16[9,640,640]{2,1,0:T(8,128)(2,1)} copy-done((bf16[9,640,640]{2,1,0:T(8,128)(2,1)}, bf16[9,640,640]{2,1,0:T(8,128)(2,1)S(1)}, u32[]{:S(2)}) %copy-start.11) | copy-done | bytes 7372824
  19.5 6.6 %all-to-all-done = bf16[16,64,320]{2,1,0:T(8,128)(2,1)S(1)} async-done(((bf16[16,64,320]{2,1,0:T(8,128)(2,1)}), bf16[16,64,320]{2,1,0:T(8,128)(2,1)S(1)}, u32[]{:S(2)}, u32[]{:S(2)}) %all-to-all-start) | async-done | bytes 655392 | tf_op jit(solution)/shard_map/all_to_all | solution.py:490
  30.9 3.2 %collective-permute-start.4 = (bf16[512,320]{1,0:T(8,128)(2,1)S(1)}, bf16[512,320]{1,0:T(8,128)(2,1)S(1)}, u32[]{:S(2)}, u32[]{:S(2)}) collective-permute-start(bf16[512,320]{1,0:T(8,128)(2,1)S(1)} %get-tuple-element.68), channel_id=1, source_target_pairs={{0,16},{16,32},{32,48},{48,64},{64,80},{80,96},{96,112},{1,17},{17... | collective-permute-start | bytes 983048 | tf_op jit(solution)/shard_map/ppermute | solution.py:482
  35.5 5.0 %collective-permute-start.3 = (f32[8,320]{1,0:T(8,128)S(1)}, f32[8,320]{1,0:T(8,128)S(1)}, u32[]{:S(2)}, u32[]{:S(2)}) collective-permute-start(f32[8,320]{1,0:T(8,128)S(1)} %add.52.refs_2_), channel_id=1, source_target_pairs={{0,96},{16,112},{32,0},{48,16},{64,32},{80,48},{96,64},{112,80},{1... | collective-permute-start | bytes 30728 | tf_op jit(solution)/shard_map/ppermute | solution.py:464
  47.6 2.8 %collective-permute-done.4.refs_2_ = bf16[512,320]{1,0:T(8,128)(2,1)S(1)} collective-permute-done((bf16[512,320]{1,0:T(8,128)(2,1)S(1)}, bf16[512,320]{1,0:T(8,128)(2,1)S(1)}, u32[]{:S(2)}, u32[]{:S(2)}) %collective-permute-start.4) | collective-permute-done | bytes 327712 | tf_op jit(solution)/shard_map/ppermute | solution.py:482
  50.5 6.1 %shard_map.111 = (bf16[384,960]{1,0:T(8,128)(2,1)S(1)}, bf16[384,960]{1,0:T(8,128)(2,1)S(1)}, bf16[128,640]{1,0:T(8,128)(2,1)S(1)}, bf16[128,640]{1,0:T(8,128)(2...) custom-call(s32[2]{0:T(128)S(1)} %add_convert_fusion.1.refs_0_, bf16[512,320]{1,0:T(8,128)(2,1)S(1)} %copy-done.17, ...), custom_call_target="tpu_custom_call" | custom-call | flops 7000000000 | bytes 1000000 | tf_op jit(solution)/shard_map/pallas_call | solution.py:120
  56.7 2.5 %shard_map.112 = (bf16[128,960]{1,0:T(8,128)(2,1)S(1)}, bf16[128,960]{1,0:T(8,128)(2,1)S(1)}, bf16[128,960]{1,0:T(8,128)(2,1)S(1)}, bf16[128,960]{1,0:T(8,128)(2,1)S(1)}, f32[128,640]{1,0:T(8,128)S(1)}) custom-call(s32[6]{0:T(128)S(1)} %stack.36.refs_0_, bf16[128,640]{1,0:T(8,128)(2,1)S(1)} %copy-done.26, ...), custom_call_target="tpu_custom_call" | custom-call | flops 6000000000 | bytes 1000000 | tf_op jit(solution)/shard_map/pallas_call | solution.py:120
  59.9 3.2 %collective-permute-start.9 = (bf16[128,960]{1,0:T(8,128)(2,1)S(1)}, bf16[128,960]{1,0:T(8,128)(2,1)S(1)}, u32[]{:S(2)}, u32[]{:S(2)}) collective-permute-start(bf16[128,960]{1,0:T(8,128)(2,1)S(1)} %get-tuple-element.80), channel_id=1, source_target_pairs={{0,4},{1,5},{2,6},{3,7},{4,0},{5,1},{6,2},{7,3},{8,12},{9,13},{10,... | collective-permute-start | bytes 737288 | tf_op jit(solution)/shard_map/ppermute | solution.py:472
  64.0 4.4 %collective-permute-start.6 = (bf16[128,320]{1,0:T(8,128)(2,1)S(1)}, bf16[128,320]{1,0:T(8,128)(2,1)S(1)}, u32[]{:S(2)}, u32[]{:S(2)}) collective-permute-start(bf16[128,320]{1,0:T(8,128)(2,1)S(1)} %get-tuple-element.76), channel_id=1, source_target_pairs={{0,16},{16,32},{32,48},{48,64},{64,80},{80,96},{96,112},{1,17},{17... | collective-permute-start | bytes 245768 | tf_op jit(solution)/shard_map/ppermute | solution.py:482
  76.1 4.1 %shard_map.117 = (bf16[320,4224]{1,0:T(8,128)(2,1)S(1)}, bf16[320,4224]{1,0:T(8,128)(2,1)S(1)}) custom-call(s32[6]{0:T(128)S(1)} %stack.36.refs_0_, bf16[640,512]{1,0:T(8,128)(2,1)S(1)} %get-tuple-element.82.refs_1_, bf16[4,640,128]{2,1,0:T(8,128)(2,1)S(1)} %get-tuple-element.83.refs_2_, bf16[640,128]{1,0:T(8,128)(2,1)S(1)} %get-tuple-element.84.refs_3_, ...), custom_call_target="tpu_custom_call" | custom-call | flops 7000000000 | bytes 1000000 | tf_op jit(solution)/shard_map/pallas_call | solution.py:120
  80.3 2.7 %shard_map.118 = (f32[512,320]{1,0:T(8,128)S(1)}, f32[8,320]{1,0:T(8,128)S(1)}) custom-call(bf16[512,320]{1,0:T(8,128)(2,1)S(1)} %copy-done.17, f32[8,320]{1,0:T(8,128)S(1)} %add_add_fusion.1.refs_4_.refs_1_, bf16[512,320]{1,0:T(8,128)(2,1)S(1)} %get-tuple-element.75.refs_1_.refs_2_, bf16[128,320]{1,0:T(8,128)(2,1)S(1)} %collective-permute-done.6.refs_8_.refs_3_, ...), custom_call_target="tpu_custom_call" | custom-call | flops 6000000000 | bytes 1000000 | tf_op jit(solution)/shard_map/pallas_call | solution.py:120
  87.4 3.9 %all-to-all-start.2 = ((bf16[4,80,4224]{2,1,0:T(8,128)(2,1)}), bf16[4,80,4224]{2,1,0:T(8,128)(2,1)S(1)}, u32[]{:S(2)}, u32[]{:S(2)}) async-start(bf16[4,80,4224]{2,1,0:T(8,128)(2,1)} %bitcast.32), calls=%async_computation.2 | async-start | bytes 5406720 | tf_op jit(solution)/shard_map/all_to_all | solution.py:500
  94.2 4.1 %shard_map.120 = (bf16[16,40,720]{2,1,0:T(8,128)(2,1)S(1)}, bf16[16,40,720]{2,1,0:T(8,128)(2,1)S(1)}) custom-call(s32[6]{0:T(128)S(1)} %stack.36.refs_0_, bf16[128,960]{1,0:T(8,128)(2,1)S(1)} %copy-done.22, bf16[128,960]{1,0:T(8,128)(2,1)S(1)} %collective-permute-done.8.refs_2_, bf16[128,960]{1,0:T(8,128)(2,1)S(1)} %copy-done.3, ...), custom_call_target="tpu_custom_call" | custom-call | flops 1000000000 | bytes 1000000 | tf_op jit(solution)/shard_map/pallas_call | solution.py:120
  98.5 2.5 %collective-permute-start.12 = (f32[8,320]{1,0:T(8,128)S(1)}, f32[8,320]{1,0:T(8,128)S(1)}, u32[]{:S(2)}, u32[]{:S(2)}) collective-permute-start(f32[8,320]{1,0:T(8,128)S(1)} %get-tuple-element.96.refs_5_), channel_id=1, source_target_pairs={{0,16},{16,0},{32,48},{48,32},{64,80},{80,64},{96,112},{112,96},{1... | collective-permute-start | bytes 30728 | tf_op jit(solution)/shard_map/ppermute | solution.py:468
  102.7 5.8 %collective-permute-start.15 = (f32[8,320]{1,0:T(8,128)S(1)}, f32[8,320]{1,0:T(8,128)S(1)}, u32[]{:S(2)}, u32[]{:S(2)}) collective-permute-start(f32[8,320]{1,0:T(8,128)S(1)} %add.61.refs_2_), channel_id=1, source_target_pairs={{0,96},{16,112},{32,0},{48,16},{64,32},{80,48},{96,64},{112,80},{1... | collective-permute-start | bytes 30728 | tf_op jit(solution)/shard_map/ppermute | solution.py:464
  115.1 4.9 %collective-permute-done.17 = bf16[4,40,720]{2,1,0:T(8,128)(2,1)S(1)} collective-permute-done((bf16[4,40,720]{2,1,0:T(8,128)(2,1)S(1)}, bf16[4,40,720]{2,1,0:T(8,128)(2,1)S(1)}, u32[]{:S(2)}, u32[]{:S(2)}) %collective-permute-start.17) | collective-permute-done | bytes 230432 | tf_op jit(solution)/shard_map/ppermute | solution.py:464
  120.0 4.3 %collective-permute-done.18 = bf16[4,40,720]{2,1,0:T(8,128)(2,1)S(1)} collective-permute-done((bf16[4,40,720]{2,1,0:T(8,128)(2,1)S(1)}, bf16[4,40,720]{2,1,0:T(8,128)(2,1)S(1)}, u32[]{:S(2)}, u32[]{:S(2)}) %collective-permute-start.18) | collective-permute-done | bytes 230432 | tf_op jit(solution)/shard_map/ppermute | solution.py:464
  126.5 5.5 %all-to-all-start.1 = ((bf16[16,64,320]{2,1,0:T(8,128)(2,1)}), bf16[16,64,320]{2,1,0:T(8,128)(2,1)}, u32[]{:S(2)}, u32[]{:S(2)}) async-start(bf16[16,64,320]{2,1,0:T(8,128)(2,1)} %copy-done.1), calls=%async_computation.1 | async-start | bytes 1572864 | tf_op jit(solution)/shard_map/all_to_all | solution.py:490
  132.1 3.3 %shard_map.123 = (bf16[2,80,640]{2,1,0:T(8,128)(2,1)S(1)}, bf16[2,80,640]{2,1,0:T(8,128)(2,1)}, bf16[2,80,640]{2,1,0:T(8,128)(2,1)}, bf16[2,80,640]{2,1,0:T(8,128)(2,1)S(1)}) custom-call(s32[6]{0:T(128)S(1)} %stack.36.refs_0_, bf16[4,80,4224]{2,1,0:T(8,128)(2,1)S(1)} %all-to-all-done.2.refs_1_, bf16[4,40,720]{2,1,0:T(8,128)(2,1)S(1)} %add_convert_fusion.refs_2_.refs_4_, ...), custom_call_target="tpu_custom_call" | custom-call | bytes 1000000 | tf_op jit(solution)/shard_map/pallas_call | solution.py:120
  137.1 2.7 %collective-permute-start.21 = (bf16[2,80,640]{2,1,0:T(8,128)(2,1)}, bf16[2,80,640]{2,1,0:T(8,128)(2,1)S(1)}, u32[]{:S(2)}, u32[]{:S(2)}) collective-permute-start(bf16[2,80,640]{2,1,0:T(8,128)(2,1)} %get-tuple-element.110), channel_id=1, source_target_pairs={{0,64},{16,80},{32,96},{48,112},{64,0},{80,16},{96,32},{112,48},{1... | collective-permute-start | bytes 614408 | tf_op jit(solution)/shard_map/ppermute | solution.py:464
  141.2 6.1 %all-to-all-done.1 = bf16[16,64,320]{2,1,0:T(8,128)(2,1)} async-done(((bf16[16,64,320]{2,1,0:T(8,128)(2,1)}), bf16[16,64,320]{2,1,0:T(8,128)(2,1)}, u32[]{:S(2)}, u32[]{:S(2)}) %all-to-all-start.1) | async-done | bytes 655392 | tf_op jit(solution)/shard_map/all_to_all | solution.py:490
  149.8 3.3 %collective-permute-start.24 = (bf16[40,1360]{1,0:T(8,128)(2,1)S(1)}, bf16[40,1360]{1,0:T(8,128)(2,1)S(1)}, u32[]{:S(2)}, u32[]{:S(2)}) collective-permute-start(bf16[40,1360]{1,0:T(8,128)(2,1)S(1)} %get-tuple-element.114), channel_id=1, source_target_pairs={{0,8},{1,9},{2,10},{3,11},{4,12},{5,13},{6,14},{7,15},{8,0},{9,1},... | collective-permute-start | bytes 326408 | tf_op jit(solution)/shard_map/ppermute | solution.py:478
  (127 shorter events, 58.4 us)
Async XLA Ops:
  2.8 23.3 %all-to-all-start = ((bf16[16,64,320]{2,1,0:T(8,128)(2,1)}), bf16[16,64,320]{2,1,0:T(8,128)(2,1)S(1)}, u32[]{:S(2)}, u32[]{:S(2)}) async-start(bf16[16,64,320]{2,1,0:T(8,128)(2,1)} %pad_maximum_fusion), calls=%async_computation | async-start | bytes 1572864 | tf_op jit(solution)/shard_map/all_to_all | solution.py:490
  30.9 19.5 %collective-permute-start.4 = (bf16[512,320]{1,0:T(8,128)(2,1)S(1)}, bf16[512,320]{1,0:T(8,128)(2,1)S(1)}, u32[]{:S(2)}, u32[]{:S(2)}) collective-permute-start(bf16[512,320]{1,0:T(8,128)(2,1)S(1)} %get-tuple-element.68), channel_id=1, source_target_pairs={{0,16},{16,32},{32,48},{48,64},{64,80},{80,96},{96,112},{1,17},{17... | collective-permute-start | bytes 983048 | tf_op jit(solution)/shard_map/ppermute | solution.py:482
  34.2 16.3 %collective-permute-start.5 = (bf16[512,320]{1,0:T(8,128)(2,1)S(1)}, bf16[512,320]{1,0:T(8,128)(2,1)S(1)}, u32[]{:S(2)}, u32[]{:S(2)}) collective-permute-start(bf16[512,320]{1,0:T(8,128)(2,1)S(1)} %get-tuple-element.69), channel_id=1, source_target_pairs={{16,0},{32,16},{48,32},{64,48},{80,64},{96,80},{112,96},{17,1},{33... | collective-permute-start | bytes 983048 | tf_op jit(solution)/shard_map/ppermute | solution.py:486
  35.5 12.1 %collective-permute-start.3 = (f32[8,320]{1,0:T(8,128)S(1)}, f32[8,320]{1,0:T(8,128)S(1)}, u32[]{:S(2)}, u32[]{:S(2)}) collective-permute-start(f32[8,320]{1,0:T(8,128)S(1)} %add.52.refs_2_), channel_id=1, source_target_pairs={{0,96},{16,112},{32,0},{48,16},{64,32},{80,48},{96,64},{112,80},{1... | collective-permute-start | bytes 30728 | tf_op jit(solution)/shard_map/ppermute | solution.py:464
  40.5 7.1 %collective-permute-start.2 = (f32[8,320]{1,0:T(8,128)S(1)}, f32[8,320]{1,0:T(8,128)S(1)}, u32[]{:S(2)}, u32[]{:S(2)}) collective-permute-start(f32[8,320]{1,0:T(8,128)S(1)} %add.52.refs_2_), channel_id=1, source_target_pairs={{0,64},{16,80},{32,96},{48,112},{64,0},{80,16},{96,32},{112,48},{1... | collective-permute-start | bytes 30728 | tf_op jit(solution)/shard_map/ppermute | solution.py:464
  59.9 12.2 %collective-permute-start.8 = (bf16[128,960]{1,0:T(8,128)(2,1)S(1)}, bf16[128,960]{1,0:T(8,128)(2,1)S(1)}, u32[]{:S(2)}, u32[]{:S(2)}) collective-permute-start(bf16[128,960]{1,0:T(8,128)(2,1)S(1)} %get-tuple-element.79), channel_id=1, source_target_pairs={{0,2},{1,3},{2,4},{3,5},{4,6},{5,7},{6,0},{7,1},{8,10},{9,11},{10,... | collective-permute-start | bytes 737288 | tf_op jit(solution)/shard_map/ppermute | solution.py:472
  59.9 14.2 %collective-permute-start.9 = (bf16[128,960]{1,0:T(8,128)(2,1)S(1)}, bf16[128,960]{1,0:T(8,128)(2,1)S(1)}, u32[]{:S(2)}, u32[]{:S(2)}) collective-permute-start(bf16[128,960]{1,0:T(8,128)(2,1)S(1)} %get-tuple-element.80), channel_id=1, source_target_pairs={{0,4},{1,5},{2,6},{3,7},{4,0},{5,1},{6,2},{7,3},{8,12},{9,13},{10,... | collective-permute-start | bytes 737288 | tf_op jit(solution)/shard_map/ppermute | solution.py:472
  63.1 11.0 %collective-permute-start.10 = (bf16[128,960]{1,0:T(8,128)(2,1)S(1)}, bf16[128,960]{1,0:T(8,128)(2,1)S(1)}, u32[]{:S(2)}, u32[]{:S(2)}) collective-permute-start(bf16[128,960]{1,0:T(8,128)(2,1)S(1)} %get-tuple-element.81), channel_id=1, source_target_pairs={{0,6},{1,7},{2,0},{3,1},{4,2},{5,3},{6,4},{7,5},{8,14},{9,15},{10,... | collective-permute-start | bytes 737288 | tf_op jit(solution)/shard_map/ppermute | solution.py:472
  64.0 12.1 %collective-permute-start.6 = (bf16[128,320]{1,0:T(8,128)(2,1)S(1)}, bf16[128,320]{1,0:T(8,128)(2,1)S(1)}, u32[]{:S(2)}, u32[]{:S(2)}) collective-permute-start(bf16[128,320]{1,0:T(8,128)(2,1)S(1)} %get-tuple-element.76), channel_id=1, source_target_pairs={{0,16},{16,32},{32,48},{48,64},{64,80},{80,96},{96,112},{1,17},{17... | collective-permute-start | bytes 245768 | tf_op jit(solution)/shard_map/ppermute | solution.py:482
  68.4 7.7 %collective-permute-start.7 = (bf16[128,320]{1,0:T(8,128)(2,1)S(1)}, bf16[128,320]{1,0:T(8,128)(2,1)S(1)}, u32[]{:S(2)}, u32[]{:S(2)}) collective-permute-start(bf16[128,320]{1,0:T(8,128)(2,1)S(1)} %get-tuple-element.77), channel_id=1, source_target_pairs={{16,0},{32,16},{48,32},{64,48},{80,64},{96,80},{112,96},{17,1},{33... | collective-permute-start | bytes 245768 | tf_op jit(solution)/shard_map/ppermute | solution.py:486
  87.4 39.1 %all-to-all-start.2 = ((bf16[4,80,4224]{2,1,0:T(8,128)(2,1)}), bf16[4,80,4224]{2,1,0:T(8,128)(2,1)S(1)}, u32[]{:S(2)}, u32[]{:S(2)}) async-start(bf16[4,80,4224]{2,1,0:T(8,128)(2,1)} %bitcast.32), calls=%async_computation.2 | async-start | bytes 5406720 | tf_op jit(solution)/shard_map/all_to_all | solution.py:500
  98.3 11.9 %collective-permute-start.16 = (bf16[16,40,720]{2,1,0:T(8,128)(2,1)S(1)}, bf16[16,40,720]{2,1,0:T(8,128)(2,1)S(1)}, u32[]{:S(2)}, u32[]{:S(2)}) collective-permute-start(bf16[16,40,720]{2,1,0:T(8,128)(2,1)S(1)} %get-tuple-element.100), channel_id=1, source_target_pairs={{0,1},{1,0},{2,3},{3,2},{4,5},{5,4},{6,7},{7,6},{8,9},{9,8},{10,11... | collective-permute-start | bytes 2764808 | tf_op jit(solution)/shard_map/ppermute | solution.py:460
  102.7 11.6 %collective-permute-start.15 = (f32[8,320]{1,0:T(8,128)S(1)}, f32[8,320]{1,0:T(8,128)S(1)}, u32[]{:S(2)}, u32[]{:S(2)}) collective-permute-start(f32[8,320]{1,0:T(8,128)S(1)} %add.61.refs_2_), channel_id=1, source_target_pairs={{0,96},{16,112},{32,0},{48,16},{64,32},{80,48},{96,64},{112,80},{1... | collective-permute-start | bytes 30728 | tf_op jit(solution)/shard_map/ppermute | solution.py:464
  108.5 6.6 %collective-permute-start.14 = (f32[8,320]{1,0:T(8,128)S(1)}, f32[8,320]{1,0:T(8,128)S(1)}, u32[]{:S(2)}, u32[]{:S(2)}) collective-permute-start(f32[8,320]{1,0:T(8,128)S(1)} %add.61.refs_2_), channel_id=1, source_target_pairs={{0,64},{16,80},{32,96},{48,112},{64,0},{80,16},{96,32},{112,48},{1... | collective-permute-start | bytes 30728 | tf_op jit(solution)/shard_map/ppermute | solution.py:464
  110.4 9.6 %collective-permute-start.17 = (bf16[4,40,720]{2,1,0:T(8,128)(2,1)S(1)}, bf16[4,40,720]{2,1,0:T(8,128)(2,1)S(1)}, u32[]{:S(2)}, u32[]{:S(2)}) collective-permute-start(bf16[4,40,720]{2,1,0:T(8,128)(2,1)S(1)} %get-tuple-element.102), channel_id=1, source_target_pairs={{0,32},{16,48},{32,64},{48,80},{64,96},{80,112},{96,0},{112,16},{1... | collective-permute-start | bytes 691208 | tf_op jit(solution)/shard_map/ppermute | solution.py:464
  112.3 12.0 %collective-permute-start.18 = (bf16[4,40,720]{2,1,0:T(8,128)(2,1)S(1)}, bf16[4,40,720]{2,1,0:T(8,128)(2,1)S(1)}, u32[]{:S(2)}, u32[]{:S(2)}) collective-permute-start(bf16[4,40,720]{2,1,0:T(8,128)(2,1)S(1)} %get-tuple-element.103), channel_id=1, source_target_pairs={{0,64},{16,80},{32,96},{48,112},{64,0},{80,16},{96,32},{112,48},{1... | collective-permute-start | bytes 691208 | tf_op jit(solution)/shard_map/ppermute | solution.py:464
  114.3 10.0 %collective-permute-start.19 = (bf16[4,40,720]{2,1,0:T(8,128)(2,1)S(1)}, bf16[4,40,720]{2,1,0:T(8,128)(2,1)S(1)}, u32[]{:S(2)}, u32[]{:S(2)}) collective-permute-start(bf16[4,40,720]{2,1,0:T(8,128)(2,1)S(1)} %get-tuple-element.104), channel_id=1, source_target_pairs={{0,96},{16,112},{32,0},{48,16},{64,32},{80,48},{96,64},{112,80},{1... | collective-permute-start | bytes 691208 | tf_op jit(solution)/shard_map/ppermute | solution.py:464
  126.5 20.8 %all-to-all-start.1 = ((bf16[16,64,320]{2,1,0:T(8,128)(2,1)}), bf16[16,64,320]{2,1,0:T(8,128)(2,1)}, u32[]{:S(2)}, u32[]{:S(2)}) async-start(bf16[16,64,320]{2,1,0:T(8,128)(2,1)} %copy-done.1), calls=%async_computation.1 | async-start | bytes 1572864 | tf_op jit(solution)/shard_map/all_to_all | solution.py:490
  135.4 12.6 %collective-permute-start.20 = (bf16[2,80,640]{2,1,0:T(8,128)(2,1)}, bf16[2,80,640]{2,1,0:T(8,128)(2,1)S(1)}, u32[]{:S(2)}, u32[]{:S(2)}) collective-permute-start(bf16[2,80,640]{2,1,0:T(8,128)(2,1)} %get-tuple-element.109), channel_id=1, source_target_pairs={{0,32},{16,48},{32,64},{48,80},{64,96},{80,112},{96,0},{112,16},{1... | collective-permute-start | bytes 614408 | tf_op jit(solution)/shard_map/ppermute | solution.py:464
  137.1 12.5 %collective-permute-start.21 = (bf16[2,80,640]{2,1,0:T(8,128)(2,1)}, bf16[2,80,640]{2,1,0:T(8,128)(2,1)S(1)}, u32[]{:S(2)}, u32[]{:S(2)}) collective-permute-start(bf16[2,80,640]{2,1,0:T(8,128)(2,1)} %get-tuple-element.110), channel_id=1, source_target_pairs={{0,64},{16,80},{32,96},{48,112},{64,0},{80,16},{96,32},{112,48},{1... | collective-permute-start | bytes 614408 | tf_op jit(solution)/shard_map/ppermute | solution.py:464
  139.8 9.8 %collective-permute-start.22 = (bf16[2,80,640]{2,1,0:T(8,128)(2,1)S(1)}, bf16[2,80,640]{2,1,0:T(8,128)(2,1)S(1)}, u32[]{:S(2)}, u32[]{:S(2)}) collective-permute-start(bf16[2,80,640]{2,1,0:T(8,128)(2,1)S(1)} %get-tuple-element.111), channel_id=1, source_target_pairs={{0,96},{16,112},{32,0},{48,16},{64,32},{80,48},{96,64},{112,80},{1... | collective-permute-start | bytes 614408 | tf_op jit(solution)/shard_map/ppermute | solution.py:464
  149.7 6.9 %collective-permute-start.23 = (bf16[40,1360]{1,0:T(8,128)(2,1)S(1)}, bf16[40,1360]{1,0:T(8,128)(2,1)S(1)}, u32[]{:S(2)}, u32[]{:S(2)}) collective-permute-start(bf16[40,1360]{1,0:T(8,128)(2,1)S(1)} %get-tuple-element.113), channel_id=1, source_target_pairs={{0,16},{16,0},{32,48},{48,32},{64,80},{80,64},{96,112},{112,96},{1... | collective-permute-start | bytes 326408 | tf_op jit(solution)/shard_map/ppermute | solution.py:468
  149.8 8.3 %collective-permute-start.24 = (bf16[40,1360]{1,0:T(8,128)(2,1)S(1)}, bf16[40,1360]{1,0:T(8,128)(2,1)S(1)}, u32[]{:S(2)}, u32[]{:S(2)}) collective-permute-start(bf16[40,1360]{1,0:T(8,128)(2,1)S(1)} %get-tuple-element.114), channel_id=1, source_target_pairs={{0,8},{1,9},{2,10},{3,11},{4,12},{5,13},{6,14},{7,15},{8,0},{9,1},... | collective-permute-start | bytes 326408 | tf_op jit(solution)/shard_map/ppermute | solution.py:478
  153.2 6.7 %collective-permute-start.25 = (bf16[40,1360]{1,0:T(8,128)(2,1)S(1)}, bf16[40,1360]{1,0:T(8,128)(2,1)S(1)}, u32[]{:S(2)}, u32[]{:S(2)}) collective-permute-start(bf16[40,1360]{1,0:T(8,128)(2,1)S(1)} %get-tuple-element.115), channel_id=1, source_target_pairs={{0,24},{1,25},{2,26},{3,27},{4,28},{5,29},{6,30},{7,31},{8,16},{9,... | collective-permute-start | bytes 326408 | tf_op jit(solution)/shard_map/ppermute | solution.py:495
  (36 other events, 212.9 us)
